TPU v7x, 512 devices: a whole 4x4x16 slice. The times are simulated.
512 devices in a mesh: grp: 4 (over z_lo), blk: 32 (over x, y, core), head: 4 (over z_hi).
Axes of the slice: x: 4, y: 4, z: 16 (z_hi: 4, z_lo: 4; z = z_hi * 4 + z_lo), core: 2. Of those that a mesh axis runs over, the one named last changes fastest.
Arguments:
- queries: bfloat16 [65536, 1024], P(('grp', 'blk', 'head')), may hold values from -6 to 6
- keys: bfloat16 [65536, 1024], P(('grp', 'blk', 'head')), may hold values from -6 to 6
- values: bfloat16 [65536, 1024], P(('grp', 'blk', 'head')), may hold values from -6 to 6
- out_grad: bfloat16 [65536, 1024], P(('grp', 'blk', 'head')), may hold values from -6 to 6
- segment: int32 [65536], P(('grp', 'blk', 'head')), may hold values from 0 to 63, never falling along the last dimension, each value on 1 to 2048 neighbouring positions
Outputs:
- attention_out: bfloat16 [65536, 1024], P(('grp', 'blk', 'head'))
- query_grad: bfloat16 [65536, 1024], P(('grp', 'blk', 'head'))
- key_grad: bfloat16 [65536, 1024], P(('grp', 'blk', 'head'))
- value_grad: bfloat16 [65536, 1024], P(('grp', 'blk', 'head'))
Inputs may be any that keep to these rules, and one draw needn't show every extreme that they name: `segment`: never falls along the pack; every stream covers 1 to 2048 consecutive positions and one covers exactly 2048.
All inputs are finite; a program needn't handle non-finite values.
Results may differ from a plain program's by a relative error of at most 0.0049.
Values may be sent and summed in bfloat16 or wider, within the bound.
A program may use at most 64 MiB of HBM per device.

v0:
```python
import functools
import math

import jax
import jax.numpy as jnp
from jax import lax
from jax.experimental import pallas as pl
from jax.experimental.pallas import tpu as pltpu
from jax.sharding import PartitionSpec as P

MESH = pl.DeviceIdType.MESH
DH = 128
REACH = 4
TOK = 128
PLANES = 4
BLOCK = TOK * PLANES
CHUNK = 2 * TOK + 16
ROWS = 256
NT = (((1,), (1,)), ((), ()))
NN = (((1,), (0,)), ((), ()))


def chip_at(grp, blk, by, blks, grps):
    chips = blks // 2
    chip = lax.rem(grp * chips + blk // 2 + by + chips * grps, chips * grps)
    return chip // chips, lax.rem(chip, chips) * 2 + lax.rem(blk, 2)


def kernel(
    sizes,
    queries, keys, values, out_grad, segment,
    out, query_grad, key_grad, value_grad,
    held, stage, result, acc, seg_rows,
    load_sem, in_send, in_recv, halo_send, halo_recv, sib_send, sib_recv, out_send, out_recv, own_sem,
):
    grps, blks = sizes
    grp, blk, me = lax.axis_index("grp"), lax.axis_index("blk"), lax.axis_index("head")
    core = lax.rem(blk, 2)
    sibling = (grp, blk + 1 - 2 * core, me)
    planes = [lax.rem(me + by, PLANES) for by in range(PLANES)]

    def along(by):
        g, b = chip_at(grp, blk, by, blks, grps)
        return (g, b, me)

    sources = ((keys, values), (queries, out_grad))
    groups = ((0, 0), (0, 1), (1, 0), (1, 1))

    def load(phase, group):
        copies = []
        for by in range(PLANES):
            plane = planes[by]
            column = pl.ds(pl.multiple_of((2 * plane + phase) * DH, DH), DH)
            for a in range(2):
                if by == 0:
                    to = held.at[phase, group, 0, me, pl.ds(a * TOK, TOK)]
                else:
                    to = stage.at[phase, group, by - 1, pl.ds(a * TOK, TOK)]
                copies.append(
                    pltpu.make_async_copy(
                        sources[group][a].at[:, column], to, load_sem.at[phase, group, by, a]
                    )
                )
        return copies

    loads = {pg: load(*pg) for pg in groups}
    for pg in groups:
        for copy in loads[pg]:
            copy.start()

    barrier = pltpu.get_barrier_semaphore()
    partners = [(grp, blk, planes[by]) for by in (1, 2, 3)]
    partners += [sibling] + [along(by) for by in (1, -1, 2, -2)]
    for partner in partners:
        pl.semaphore_signal(barrier, inc=1, device_id=partner, device_id_type=MESH)

    seg = jnp.broadcast_to(segment[...].astype(jnp.float32), (16, TOK)).astype(jnp.bfloat16)
    for by in range(3):
        stage[0, 0, by, 2 * TOK :, :] = seg
    held[0, 0, 0, me, 2 * TOK :, :] = seg

    pl.semaphore_wait(barrier, len(partners))

    def rows_sent(phase, group):
        return CHUNK if (phase, group) == (0, 0) else 2 * TOK

    def exchange(phase, group):
        rows = pl.ds(0, rows_sent(phase, group))
        return [
            pltpu.make_async_remote_copy(
                src_ref=stage.at[phase, group, by - 1, rows],
                dst_ref=held.at[phase, group, 0, me, rows],
                send_sem=in_send.at[phase, group, by - 1],
                recv_sem=in_recv.at[phase, group, by - 1],
                device_id=(grp, blk, planes[by]),
                device_id_type=MESH,
            )
            for by in (2, 1, 3)
        ]

    def halo(phase, group):
        rows = pl.ds(0, CHUNK if phase == 0 else 2 * TOK)
        way = 1 - 2 * group
        return [
            pltpu.make_async_remote_copy(
                src_ref=held.at[phase, group, 0, :, rows],
                dst_ref=held.at[phase, group, 2 * by, :, rows],
                send_sem=halo_send.at[phase, group, by - 1],
                recv_sem=halo_recv.at[phase, group, by - 1],
                device_id=along(by * way),
                device_id_type=MESH,
            )
            for by in (1, 2)
        ]

    def share(phase, group):
        rows = pl.ds(0, CHUNK if phase == 0 else 2 * TOK)
        side = core if group == 0 else 1 - core
        return [
            pltpu.make_async_remote_copy(
                src_ref=held.at[phase, group, 2 * j + 2 * side, :, rows],
                dst_ref=held.at[phase, group, 2 * j + 1, :, rows],
                send_sem=sib_send.at[phase, group, j],
                recv_sem=sib_recv.at[phase, group, j],
                device_id=sibling,
                device_id_type=MESH,
            )
            for j in range(2)
        ]

    targets = ((query_grad, out), (key_grad, value_grad))

    def give(phase, group):
        column = pl.ds(pl.multiple_of((2 * me + phase) * DH, DH), DH)
        copies = []
        for by in (2, 1, 3):
            for a in range(2):
                copies.append(
                    pltpu.make_async_remote_copy(
                        src_ref=result.at[phase, group, a, planes[by]],
                        dst_ref=targets[group][a].at[:, column],
                        send_sem=out_send.at[phase, group, a, by - 1],
                        recv_sem=out_recv.at[phase, group, a, by - 1],
                        device_id=(grp, blk, planes[by]),
                        device_id_type=MESH,
                    )
                )
        own = [
            pltpu.make_async_copy(
                result.at[phase, group, a, me],
                targets[group][a].at[:, column],
                own_sem.at[phase, group, a],
            )
            for a in range(2)
        ]
        return copies, own

    score_scale = 1.0 / math.sqrt(DH)
    norm = 1.0 / math.sqrt(REACH * BLOCK)
    part = ROWS // TOK

    def unit(phase, group, slot, step, diagonal):
        mine = held.at[phase, 1 - group, 0, pl.ds(step * part, part)]
        theirs = held.at[phase, group, slot]
        first = mine[:, 0:TOK, :].reshape(ROWS, DH)
        second = mine[:, TOK : 2 * TOK, :].reshape(ROWS, DH)
        other_first = theirs[:, 0:TOK, :].reshape(BLOCK, DH)
        other_second = theirs[:, TOK : 2 * TOK, :].reshape(BLOCK, DH)
        their_seg = held[0, group, slot, :, 2 * TOK :, :].astype(jnp.float32)
        at = pl.ds(pl.multiple_of(step * ROWS, ROWS), ROWS)
        my_seg = seg_rows[at, :]
        scores = lax.dot_general(first, other_first, NT, preferred_element_type=jnp.float32)
        dprob = lax.dot_general(second, other_second, NT, preferred_element_type=jnp.float32)
        weights, dscores = [], []
        for p in range(PLANES):
            cols = slice(p * TOK, (p + 1) * TOK)
            allowed = my_seg == their_seg[p, 0:1, :]
            if diagonal:
                row = lax.broadcasted_iota(jnp.int32, (ROWS, TOK), 0) + step * ROWS
                col = lax.broadcasted_iota(jnp.int32, (ROWS, TOK), 1) + p * TOK
                allowed = allowed & ((col <= row) if group == 0 else (row <= col))
            v = scores[:, cols] * score_scale
            s = 1.0 / (1.0 + jnp.exp(-v))
            active = v * s
            slope = s + active * (1.0 - s)
            weights.append(jnp.where(allowed, active * norm, 0.0).astype(jnp.bfloat16))
            dscores.append(
                jnp.where(allowed, dprob[:, cols] * slope * (norm * score_scale), 0.0).astype(
                    jnp.bfloat16
                )
            )
        weight = jnp.concatenate(weights, axis=1)
        dscore = jnp.concatenate(dscores, axis=1)
        first_term = lax.dot_general(dscore, other_first, NN, preferred_element_type=jnp.float32)
        second_term = lax.dot_general(weight, other_second, NN, preferred_element_type=jnp.float32)
        if diagonal:
            acc[group, 0, at, :] = first_term
            acc[group, 1, at, :] = second_term
        else:
            acc[group, 0, at, :] += first_term
            acc[group, 1, at, :] += second_term

    steps = BLOCK // ROWS

    def diagonal(phase, group):
        def body(step, carry):
            unit(phase, group, 0, step, True)
            return carry

        lax.fori_loop(0, steps, body, 0)

    def others(phase, group):
        def body(i, carry):
            unit(phase, group, 1 + i // steps, lax.rem(i, steps), False)
            return carry

        lax.fori_loop(0, REACH * steps, body, 0)

    def finish(phase, group):
        for a in range(2):
            for p in range(PLANES):
                result[phase, group, a, p] = acc[group, a, p * TOK : (p + 1) * TOK, :].astype(
                    jnp.bfloat16
                )

    sent = []
    exchanges = {pg: exchange(*pg) for pg in groups}
    halos = {pg: halo(*pg) for pg in groups}
    shares = {pg: share(*pg) for pg in groups}
    gives = {pg: give(*pg) for pg in groups}

    def start_exchange(pg):
        for copy in loads[pg]:
            copy.wait()
        for copy in exchanges[pg]:
            copy.start()

    def arrive(pg):
        for copy in exchanges[pg]:
            copy.wait_recv()

    def start_halo(pg):
        for copy in halos[pg]:
            copy.start()

    def finish_halo(pg):
        for halo_copy, share_copy in zip(halos[pg], shares[pg]):
            halo_copy.wait_recv()
            share_copy.start()
        for share_copy in shares[pg]:
            share_copy.wait_recv()

    def start_give(pg):
        remote, own = gives[pg]
        for copy in remote + own:
            copy.start()

    kv_a, qd_a, kv_b, qd_b = groups
    start_exchange(kv_a)
    start_exchange(qd_a)

    arrive(kv_a)
    start_halo(kv_a)
    start_exchange(kv_b)
    for p in range(PLANES):
        row = held[0, 0, 0, p, 2 * TOK :, :].astype(jnp.float32)[0:1, :]
        seg_rows[p * TOK : (p + 1) * TOK, :] = jnp.broadcast_to(row, (TOK, TOK)).T
        held[0, 1, 0, p, 2 * TOK :, :] = held[0, 0, 0, p, 2 * TOK :, :]

    arrive(qd_a)
    start_halo(qd_a)
    start_exchange(qd_b)
    diagonal(0, 0)
    finish_halo(kv_a)
    others(0, 0)
    finish(0, 0)
    start_give(kv_a)

    arrive(kv_b)
    start_halo(kv_b)
    diagonal(0, 1)
    finish_halo(qd_a)
    others(0, 1)
    finish(0, 1)
    start_give(qd_a)

    arrive(qd_b)
    start_halo(qd_b)
    diagonal(1, 0)
    finish_halo(kv_b)
    others(1, 0)
    finish(1, 0)
    start_give(kv_b)

    diagonal(1, 1)
    finish_halo(qd_b)
    others(1, 1)
    finish(1, 1)
    start_give(qd_b)

    for pg in groups:
        for copy in exchanges[pg] + halos[pg] + shares[pg]:
            copy.wait_send()
    for pg in groups:
        remote, own = gives[pg]
        for copy in remote:
            copy.wait()
        for copy in own:
            copy.wait()


def shards(sizes, queries, keys, values, out_grad, segment):
    tokens, features = queries.shape
    shape = jax.ShapeDtypeStruct((tokens, features), jnp.bfloat16)
    anywhere = pl.BlockSpec(memory_space=pl.ANY)
    dma = pltpu.SemaphoreType.DMA
    return pl.pallas_call(
        functools.partial(kernel, sizes),
        out_shape=(shape,) * 4,
        in_specs=[anywhere] * 4 + [pl.BlockSpec(memory_space=pltpu.VMEM)],
        out_specs=[anywhere] * 4,
        scratch_shapes=[
            pltpu.VMEM((2, 2, REACH + 1, PLANES, CHUNK, DH), jnp.bfloat16),
            pltpu.VMEM((2, 2, PLANES - 1, CHUNK, DH), jnp.bfloat16),
            pltpu.VMEM((2, 2, 2, PLANES, TOK, DH), jnp.bfloat16),
            pltpu.VMEM((2, 2, BLOCK, DH), jnp.float32),
            pltpu.VMEM((BLOCK, TOK), jnp.float32),
            dma((2, 2, PLANES, 2)),
            dma((2, 2, 3)),
            dma((2, 2, 3)),
            dma((2, 2, 2)),
            dma((2, 2, 2)),
            dma((2, 2, 2)),
            dma((2, 2, 2)),
            dma((2, 2, 2, 3)),
            dma((2, 2, 2, 3)),
            dma((2, 2, 2)),
        ],
        compiler_params=pltpu.CompilerParams(
            collective_id=0, has_side_effects=True, vmem_limit_bytes=48 << 20
        ),
        cost_estimate=pl.CostEstimate(
            flops=2 * 2 * 10 * 4 * BLOCK * BLOCK * DH,
            bytes_accessed=8 * tokens * features * 2,
            transcendentals=2 * 10 * BLOCK * BLOCK,
        ),
    )(queries, keys, values, out_grad, segment.reshape(1, tokens))


def solution(mesh):
    rows = P(("grp", "blk", "head"), None)
    return jax.shard_map(
        functools.partial(shards, (mesh.shape["grp"], mesh.shape["blk"])),
        mesh=mesh,
        in_specs=(rows, rows, rows, rows, P(("grp", "blk", "head"))),
        out_specs=(rows,) * 4,
        check_vma=False,
    )
```

profile of v0, /device:TPU:104, one launch (start us, length us, event | category | flops | bytes accessed | tf_op | source)
XLA Modules:
  0.0 164.5 jit_solution(14385013692305116422)
XLA Ops:
  0.6 0.0 copy-start.4
  0.6 0.6 copy-done.4
  1.3 0.0 copy-start
  1.3 0.9 copy-done
  2.2 0.0 copy-start.1
  2.2 0.9 copy-done.1
  3.2 0.0 copy-start.2
  3.2 0.9 copy-done.2
  4.1 0.0 copy-start.3
  4.1 0.9 copy-done.3
  5.1 156.6 %shard_map.84 = (bf16[128,1024]{1,0:T(8,128)(2,1)S(1)}, bf16[128,1024]{1,0:T(8,128)(2,1)S(1)}, bf16[128,1024]{1,0:T(8,128)(2,1)S(1)}, bf16[128,1024]{1,0:T(8,128)(2,1)S(1)}) custom-call(bf16[128,1024]{1,0:T(8,128)(2,1)S(1)} %copy-done, bf16[128,1024]{1,0:T(8,128)(2,1)S(1)} %copy-done.1, bf16[128,1024]{1,0:T(8,128)(2,1)S(1)} %copy-done.2, ...), custom_call_target="tpu_custom_call" | custom-call | flops 5368709120 | bytes 2097152 | tf_op jit(solution)/shard_map/pallas_call | solution.py:317
  161.7 0.7 copy.13
  162.4 0.7 copy.14
  163.1 0.7 copy.15
  163.8 0.7 copy.16
Async XLA Ops:
  0.6 0.7 copy-start.4
  1.3 0.9 copy-start
  2.2 0.9 copy-start.1
  3.2 0.9 copy-start.2
  4.1 0.9 copy-start.3
where the time goes:
time: 165 us
  Pallas kernels  157 us (95%)
  local copies, waits for them, and re-layouts  7.26 us (4%)
    pallas_call x1, Pallas kernels, shards(): pl.pallas_call(functools.partial(kernel, sizes), out_shape=(shape,) * 4,...  157 us
    unnamed x14, local copies, waits for them, and re-layouts  7.26 us

commit v1 on v0

--- a/solution.py
+++ b/solution.py
@@ -20,28 +20,41 @@
 NN = (((1,), (0,)), ((), ()))
 
 
-def chip_at(grp, blk, by, blks, grps):
-    chips = blks // 2
-    chip = lax.rem(grp * chips + blk // 2 + by + chips * grps, chips * grps)
-    return chip // chips, lax.rem(chip, chips) * 2 + lax.rem(blk, 2)
+SIDE = 4
+CHIPS = SIDE * SIDE
 
 
 def kernel(
-    sizes,
+    grps,
     queries, keys, values, out_grad, segment,
     out, query_grad, key_grad, value_grad,
     held, stage, result, acc, seg_rows,
     load_sem, in_send, in_recv, halo_send, halo_recv, sib_send, sib_recv, out_send, out_recv, own_sem,
+    relay, piece_send, relay_recv, relay_send, next_send, seg_sem, seg_here,
 ):
-    grps, blks = sizes
     grp, blk, me = lax.axis_index("grp"), lax.axis_index("blk"), lax.axis_index("head")
     core = lax.rem(blk, 2)
     sibling = (grp, blk + 1 - 2 * core, me)
     planes = [lax.rem(me + by, PLANES) for by in range(PLANES)]
 
-    def along(by):
-        g, b = chip_at(grp, blk, by, blks, grps)
-        return (g, b, me)
+    def mirrored(group, place):
+        g, x, y = place
+        return place if group else (grps - 1 - g, SIDE - 1 - x, SIDE - 1 - y)
+
+    def device(group, place):
+        g, x, y = mirrored(group, place)
+        return (g, (x * SIDE + y) * 2 + core, me)
+
+    here = (grp, blk // (2 * SIDE), lax.rem(blk // 2, SIDE))
+
+    def chip(group):
+        g, x, y = mirrored(group, here)
+        return g, x, y, x * SIDE + y
+
+    def chip_place(g, k):
+        return g, k // SIDE, lax.rem(k, SIDE)
+
+    last = (SIDE - 1, SIDE - 1)
 
     sources = ((keys, values), (queries, out_grad))
     groups = ((0, 0), (0, 1), (1, 0), (1, 1))
@@ -68,18 +81,65 @@
         for copy in loads[pg]:
             copy.start()
 
+    seg_load = pltpu.make_async_copy(segment, seg_here, seg_sem)
+    seg_load.start()
+
     barrier = pltpu.get_barrier_semaphore()
-    partners = [(grp, blk, planes[by]) for by in (1, 2, 3)]
-    partners += [sibling] + [along(by) for by in (1, -1, 2, -2)]
-    for partner in partners:
-        pl.semaphore_signal(barrier, inc=1, device_id=partner, device_id_type=MESH)
-
-    seg = jnp.broadcast_to(segment[...].astype(jnp.float32), (16, TOK)).astype(jnp.bfloat16)
+
+    def greet(to):
+        pl.semaphore_signal(barrier, inc=1, device_id=to, device_id_type=MESH)
+
+    for by in range(1, PLANES):
+        greet((grp, blk, planes[by]))
+    greet(sibling)
+    greeted = PLANES
+
+    def greet_if(condition, partners):
+        @pl.when(condition)
+        def _():
+            for partner in partners:
+                greet(partner)
+
+        return jnp.where(condition, len(partners), 0)
+
+    for group in range(2):
+        g, x, y, k = chip(group)
+        for by in (1, 2):
+            greeted += greet_if(k >= by, [device(group, chip_place(g, k - by))])
+            greeted += greet_if(k < CHIPS - by, [device(group, chip_place(g, k + by))])
+        relays = (y <= 1) & (g >= 1)
+        greeted += greet_if(
+            relays & (x == 0), [device(group, (g, p, y)) for p in range(1, SIDE)]
+        )
+        greeted += greet_if(relays & (x > 0), [device(group, (g, 0, y))])
+        greeted += greet_if(relays, [device(group, (g - 1, *last))])
+        greeted += greet_if(
+            (k == CHIPS - 1) & (g < grps - 1),
+            [device(group, (g + 1, p, row)) for p in range(SIDE) for row in range(2)],
+        )
+
+    def blank(group, slot):
+        for phase in range(2):
+            held[phase, group, slot, :, 0 : 2 * TOK, :] = jnp.zeros(
+                (PLANES, 2 * TOK, DH), jnp.bfloat16
+            )
+        held[0, group, slot, :, 2 * TOK :, :] = jnp.full((PLANES, 16, DH), -1, jnp.bfloat16)
+
+    def comes(group, by):
+        g, x, y, k = chip(group)
+        return (g < grps - 1) | (k < CHIPS - by)
+
+    for group in range(2):
+        for by in (1, 2):
+            pl.when(~comes(group, by))(functools.partial(blank, group, 2 * by))
+
+    seg_load.wait()
+    seg = jnp.broadcast_to(seg_here[...].astype(jnp.float32), (16, TOK)).astype(jnp.bfloat16)
     for by in range(3):
         stage[0, 0, by, 2 * TOK :, :] = seg
     held[0, 0, 0, me, 2 * TOK :, :] = seg
 
-    pl.semaphore_wait(barrier, len(partners))
+    pl.semaphore_wait(barrier, greeted)
 
     def rows_sent(phase, group):
         return CHUNK if (phase, group) == (0, 0) else 2 * TOK
@@ -98,23 +158,84 @@
             for by in (2, 1, 3)
         ]
 
+    def block_rows(phase):
+        return pl.ds(0, CHUNK if phase == 0 else 2 * TOK)
+
+    def send(source, to, send_sem, recv_sem, device_id):
+        return pltpu.make_async_remote_copy(
+            src_ref=source,
+            dst_ref=to,
+            send_sem=send_sem,
+            recv_sem=recv_sem,
+            device_id=device_id,
+            device_id_type=MESH,
+        )
+
     def halo(phase, group):
-        rows = pl.ds(0, CHUNK if phase == 0 else 2 * TOK)
-        way = 1 - 2 * group
-        return [
-            pltpu.make_async_remote_copy(
-                src_ref=held.at[phase, group, 0, :, rows],
-                dst_ref=held.at[phase, group, 2 * by, :, rows],
-                send_sem=halo_send.at[phase, group, by - 1],
-                recv_sem=halo_recv.at[phase, group, by - 1],
-                device_id=along(by * way),
-                device_id_type=MESH,
-            )
-            for by in (1, 2)
-        ]
+        rows = block_rows(phase)
+        g, x, y, k = chip(group)
+        copies = []
+        for by in (1, 2):
+            copies.append((
+                k >= by,
+                send(
+                    held.at[phase, group, 0, :, rows],
+                    held.at[phase, group, 2 * by, :, rows],
+                    halo_send.at[phase, group, by - 1],
+                    halo_recv.at[phase, group, by - 1],
+                    device(group, chip_place(g, jnp.maximum(k - by, 0))),
+                ),
+            ))
+        edge = (k <= 1) & (g >= 1)
+        near_row = jnp.minimum(y, 1)
+        for p in range(1, SIDE):
+            copies.append((
+                edge,
+                send(
+                    held.at[phase, group, 0, p, rows],
+                    relay.at[phase, group, rows],
+                    piece_send.at[phase, group, p],
+                    relay_recv.at[phase, group],
+                    device(group, (g, p, y)),
+                ),
+            ))
+        copies.append((
+            edge,
+            send(
+                held.at[phase, group, 0, 0, rows],
+                held.at[phase, group, 2 * (near_row + 1), 0, rows],
+                piece_send.at[phase, group, 0],
+                halo_recv.at[phase, group, near_row],
+                device(group, (jnp.maximum(g - 1, 0), *last)),
+            ),
+        ))
+        return copies
+
+    def pass_piece(phase, group):
+        rows = block_rows(phase)
+        g, x, y, k = chip(group)
+        near_row = jnp.minimum(y, 1)
+        return (x >= 1) & (y <= 1) & (g >= 1), send(
+            relay.at[phase, group, rows],
+            held.at[phase, group, 2 * (near_row + 1), x, rows],
+            relay_send.at[phase, group],
+            halo_recv.at[phase, group, near_row],
+            device(group, (jnp.maximum(g - 1, 0), *last)),
+        )
+
+    def pass_block(phase, group):
+        rows = block_rows(phase)
+        g, x, y, k = chip(group)
+        return (k == CHIPS - 1) & (g < grps - 1), send(
+            held.at[phase, group, 2, :, rows],
+            held.at[phase, group, 4, :, rows],
+            next_send.at[phase, group],
+            halo_recv.at[phase, group, 1],
+            device(group, (g, SIDE - 1, SIDE - 2)),
+        )
 
     def share(phase, group):
-        rows = pl.ds(0, CHUNK if phase == 0 else 2 * TOK)
+        rows = block_rows(phase)
         side = core if group == 0 else 1 - core
         return [
             pltpu.make_async_remote_copy(
@@ -223,9 +344,10 @@
                     jnp.bfloat16
                 )
 
-    sent = []
     exchanges = {pg: exchange(*pg) for pg in groups}
     halos = {pg: halo(*pg) for pg in groups}
+    passed = {pg: pass_piece(*pg) for pg in groups}
+    seconds = {pg: pass_block(*pg) for pg in groups}
     shares = {pg: share(*pg) for pg in groups}
     gives = {pg: give(*pg) for pg in groups}
 
@@ -240,17 +362,31 @@
             copy.wait_recv()
 
     def start_halo(pg):
-        for copy in halos[pg]:
+        for condition, copy in halos[pg]:
+            pl.when(condition)(copy.start)
+
+    def hand_on(pg):
+        condition, copy = passed[pg]
+
+        @pl.when(condition)
+        def _():
+            pltpu.make_async_copy(copy.src_ref, copy.src_ref, relay_recv.at[pg]).wait()
             copy.start()
 
-    def finish_halo(pg):
-        for halo_copy, share_copy in zip(halos[pg], shares[pg]):
-            halo_copy.wait_recv()
-            share_copy.start()
-        for share_copy in shares[pg]:
-            share_copy.wait_recv()
+    def near(pg):
+        pl.when(comes(pg[1], 1))(halos[pg][0][1].wait_recv)
+        condition, copy = seconds[pg]
+        pl.when(condition)(copy.start)
+        shares[pg][0].start()
+
+    def far(pg):
+        pl.when(comes(pg[1], 2))(halos[pg][1][1].wait_recv)
+        shares[pg][1].start()
+        for copy in shares[pg]:
+            copy.wait_recv()
 
     def start_give(pg):
+        finish(*pg)
         remote, own = gives[pg]
         for copy in remote + own:
             copy.start()
@@ -266,58 +402,70 @@
         row = held[0, 0, 0, p, 2 * TOK :, :].astype(jnp.float32)[0:1, :]
         seg_rows[p * TOK : (p + 1) * TOK, :] = jnp.broadcast_to(row, (TOK, TOK)).T
         held[0, 1, 0, p, 2 * TOK :, :] = held[0, 0, 0, p, 2 * TOK :, :]
+    hand_on(kv_a)
+    near(kv_a)
 
     arrive(qd_a)
     start_halo(qd_a)
     start_exchange(qd_b)
-    diagonal(0, 0)
-    finish_halo(kv_a)
-    others(0, 0)
-    finish(0, 0)
+    diagonal(*kv_a)
+    far(kv_a)
+    hand_on(qd_a)
+    others(*kv_a)
     start_give(kv_a)
+    near(qd_a)
+    diagonal(*qd_a)
+    far(qd_a)
+    others(*qd_a)
+    start_give(qd_a)
 
     arrive(kv_b)
     start_halo(kv_b)
-    diagonal(0, 1)
-    finish_halo(qd_a)
-    others(0, 1)
-    finish(0, 1)
-    start_give(qd_a)
-
+    hand_on(kv_b)
+    near(kv_b)
     arrive(qd_b)
     start_halo(qd_b)
-    diagonal(1, 0)
-    finish_halo(kv_b)
-    others(1, 0)
-    finish(1, 0)
+    diagonal(*kv_b)
+    far(kv_b)
+    hand_on(qd_b)
+    others(*kv_b)
     start_give(kv_b)
-
-    diagonal(1, 1)
-    finish_halo(qd_b)
-    others(1, 1)
-    finish(1, 1)
+    near(qd_b)
+    diagonal(*qd_b)
+    far(qd_b)
+    others(*qd_b)
     start_give(qd_b)
 
     for pg in groups:
-        for copy in exchanges[pg] + halos[pg] + shares[pg]:
+        for copy in exchanges[pg] + shares[pg]:
             copy.wait_send()
+        for condition, copy in halos[pg] + [passed[pg], seconds[pg]]:
+            pl.when(condition)(copy.wait_send)
     for pg in groups:
         remote, own = gives[pg]
-        for copy in remote:
+        for copy in remote + own:
             copy.wait()
-        for copy in own:
-            copy.wait()
-
-
-def shards(sizes, queries, keys, values, out_grad, segment):
+
+
+def hand_over(*refs):
+    copies = [
+        pltpu.make_async_copy(refs[i], refs[4 + i], refs[8].at[i]) for i in range(4)
+    ]
+    for copy in copies:
+        copy.start()
+    for copy in copies:
+        copy.wait()
+
+
+def shards(grps, queries, keys, values, out_grad, segment):
     tokens, features = queries.shape
     shape = jax.ShapeDtypeStruct((tokens, features), jnp.bfloat16)
     anywhere = pl.BlockSpec(memory_space=pl.ANY)
     dma = pltpu.SemaphoreType.DMA
-    return pl.pallas_call(
-        functools.partial(kernel, sizes),
+    results = pl.pallas_call(
+        functools.partial(kernel, grps),
         out_shape=(shape,) * 4,
-        in_specs=[anywhere] * 4 + [pl.BlockSpec(memory_space=pltpu.VMEM)],
+        in_specs=[anywhere] * 5,
         out_specs=[anywhere] * 4,
         scratch_shapes=[
             pltpu.VMEM((2, 2, REACH + 1, PLANES, CHUNK, DH), jnp.bfloat16),
@@ -335,9 +483,16 @@
             dma((2, 2, 2, 3)),
             dma((2, 2, 2, 3)),
             dma((2, 2, 2)),
+            pltpu.VMEM((2, 2, CHUNK, DH), jnp.bfloat16),
+            dma((2, 2, SIDE)),
+            dma((2, 2)),
+            dma((2, 2)),
+            dma((2, 2)),
+            dma(()),
+            pltpu.VMEM((1, TOK), jnp.int32),
         ],
         compiler_params=pltpu.CompilerParams(
-            collective_id=0, has_side_effects=True, vmem_limit_bytes=48 << 20
+            collective_id=0, has_side_effects=True, vmem_limit_bytes=60 << 20
         ),
         cost_estimate=pl.CostEstimate(
             flops=2 * 2 * 10 * 4 * BLOCK * BLOCK * DH,
@@ -345,12 +500,20 @@
             transcendentals=2 * 10 * BLOCK * BLOCK,
         ),
     )(queries, keys, values, out_grad, segment.reshape(1, tokens))
+    return pl.pallas_call(
+        hand_over,
+        out_shape=(shape,) * 4,
+        in_specs=[anywhere] * 4,
+        out_specs=[anywhere] * 4,
+        scratch_shapes=[dma((4,))],
+        compiler_params=pltpu.CompilerParams(vmem_limit_bytes=60 << 20),
+    )(*results)
 
 
 def solution(mesh):
     rows = P(("grp", "blk", "head"), None)
     return jax.shard_map(
-        functools.partial(shards, (mesh.shape["grp"], mesh.shape["blk"])),
+        functools.partial(shards, mesh.shape["grp"]),
         mesh=mesh,
         in_specs=(rows, rows, rows, rows, P(("grp", "blk", "head"))),
         out_specs=(rows,) * 4,

time: 165 us -> 183 us (1.11)
  the two profiles are of different devices: /device:TPU:104 before, /device:TPU:55 now
where the time goes in v1:
time: 183 us; the launch traced here: 182 us
  Pallas kernels  182 us (99%)
    pallas_call x1, Pallas kernels, shards(): pl.pallas_call(functools.partial(kernel, grps), out_shape=(shape,) * 4, i...  149 us
    pallas_call x1, Pallas kernels, shards(): pl.pallas_call(hand_over, out_shape=(shape,) * 4, in_specs=[anywhere] * 4...  32.9 us

profile of v1, /device:TPU:55, one launch (start us, length us, event | category | flops | bytes accessed | tf_op | source)
XLA Modules:
  0.0 182.4 jit_solution(6273351684207836134)
XLA Ops:
  0.6 148.8 %shard_map.84 = (bf16[128,1024]{1,0:T(8,128)(2,1)}, bf16[128,1024]{1,0:T(8,128)(2,1)}, bf16[128,1024]{1,0:T(8,128)(2,1)}, bf16[128,1024]{1,0:T(8,128)(2,1)}) custom-call(bf16[128,1024]{1,0:T(8,128)(2,1)} %queries.1, bf16[128,1024]{1,0:T(8,128)(2,1)} %keys.1, bf16[128,1024]{1,0:T(8,128)(2,1)} %values.1, bf16[128,1024]{1,0:T(8,128)(2,1)} %out_grad.1, ...), custom_call_target="tpu_custom_call" | custom-call | flops 5368709120 | bytes 2097152 | tf_op jit(solution)/shard_map/pallas_call | solution.py:465
  149.5 32.9 %shard_map.85 = (bf16[128,1024]{1,0:T(8,128)(2,1)}, bf16[128,1024]{1,0:T(8,128)(2,1)}, bf16[128,1024]{1,0:T(8,128)(2,1)}, bf16[128,1024]{1,0:T(8,128)(2,1)}) custom-call(bf16[128,1024]{1,0:T(8,128)(2,1)} %get-tuple-element.8.refs_0_, bf16[128,1024]{1,0:T(8,128)(2,1)} %get-tuple-element.9.refs_1_, bf16[128,1024]{1,0:T(8,128)(2,1)} %get-tuple-element.10.refs_2_, ...), custom_call_target="tpu_custom_call" | custom-call | tf_op jit(solution)/shard_map/pallas_call | solution.py:503

commit v2 on v1

--- a/solution.py
+++ b/solution.py
@@ -9,13 +9,16 @@
 from jax.sharding import PartitionSpec as P
 
 MESH = pl.DeviceIdType.MESH
+LOG2E = math.log2(math.e)
 DH = 128
 REACH = 4
 TOK = 128
 PLANES = 4
 BLOCK = TOK * PLANES
 CHUNK = 2 * TOK + 16
-ROWS = 256
+PART = 64
+PARTS = 2 * TOK // PART
+ROWS = 512
 NT = (((1,), (1,)), ((), ()))
 NN = (((1,), (0,)), ((), ()))
 
@@ -38,8 +41,10 @@
     planes = [lax.rem(me + by, PLANES) for by in range(PLANES)]
 
     def mirrored(group, place):
-        g, x, y = place
-        return place if group else (grps - 1 - g, SIDE - 1 - x, SIDE - 1 - y)
+        turned = [n - 1 - at for n, at in zip((grps, SIDE, SIDE), place)]
+        if isinstance(group, int):
+            return tuple(place if group else turned)
+        return tuple(jnp.where(group == 1, *pair) for pair in zip(place, turned))
 
     def device(group, place):
         g, x, y = mirrored(group, place)
@@ -55,6 +60,9 @@
         return g, k // SIDE, lax.rem(k, SIDE)
 
     last = (SIDE - 1, SIDE - 1)
+
+    first = jnp.where(chip(1)[3] <= 1, 1, 0)
+    order = (first, 1 - first)
 
     sources = ((keys, values), (queries, out_grad))
     groups = ((0, 0), (0, 1), (1, 0), (1, 1))
@@ -135,28 +143,31 @@
 
     seg_load.wait()
     seg = jnp.broadcast_to(seg_here[...].astype(jnp.float32), (16, TOK)).astype(jnp.bfloat16)
-    for by in range(3):
-        stage[0, 0, by, 2 * TOK :, :] = seg
-    held[0, 0, 0, me, 2 * TOK :, :] = seg
+    for group in range(2):
+        for by in range(3):
+            stage[0, group, by, 2 * TOK :, :] = seg
+        held[0, group, 0, me, 2 * TOK :, :] = seg
 
     pl.semaphore_wait(barrier, greeted)
 
-    def rows_sent(phase, group):
-        return CHUNK if (phase, group) == (0, 0) else 2 * TOK
-
-    def exchange(phase, group):
-        rows = pl.ds(0, rows_sent(phase, group))
-        return [
-            pltpu.make_async_remote_copy(
-                src_ref=stage.at[phase, group, by - 1, rows],
-                dst_ref=held.at[phase, group, 0, me, rows],
-                send_sem=in_send.at[phase, group, by - 1],
-                recv_sem=in_recv.at[phase, group, by - 1],
-                device_id=(grp, blk, planes[by]),
-                device_id_type=MESH,
-            )
-            for by in (2, 1, 3)
-        ]
+    def exchange(phase, turn):
+        group = order[turn]
+        total = CHUNK if phase == turn == 0 else 2 * TOK
+        parts = []
+        for n in range(PARTS):
+            rows = pl.ds(n * PART, total - n * PART if n == PARTS - 1 else PART)
+            parts.append([
+                pltpu.make_async_remote_copy(
+                    src_ref=stage.at[phase, group, by - 1, rows],
+                    dst_ref=held.at[phase, group, 0, me, rows],
+                    send_sem=in_send.at[phase, group, n, by - 1],
+                    recv_sem=in_recv.at[phase, group, n, by - 1],
+                    device_id=(grp, blk, planes[by]),
+                    device_id_type=MESH,
+                )
+                for by in (2, 1, 3)
+            ])
+        return parts
 
     def block_rows(phase):
         return pl.ds(0, CHUNK if phase == 0 else 2 * TOK)
@@ -253,19 +264,20 @@
 
     def give(phase, group):
         column = pl.ds(pl.multiple_of((2 * me + phase) * DH, DH), DH)
-        copies = []
-        for by in (2, 1, 3):
-            for a in range(2):
-                copies.append(
-                    pltpu.make_async_remote_copy(
-                        src_ref=result.at[phase, group, a, planes[by]],
-                        dst_ref=targets[group][a].at[:, column],
-                        send_sem=out_send.at[phase, group, a, by - 1],
-                        recv_sem=out_recv.at[phase, group, a, by - 1],
-                        device_id=(grp, blk, planes[by]),
-                        device_id_type=MESH,
-                    )
+        parts = []
+        for n in range(PARTS):
+            a, rows = n * PART // TOK, pl.ds(n * PART % TOK, PART)
+            parts.append([
+                pltpu.make_async_remote_copy(
+                    src_ref=result.at[phase, group, a, planes[by], rows],
+                    dst_ref=targets[group][a].at[rows, column],
+                    send_sem=out_send.at[phase, group, n, by - 1],
+                    recv_sem=out_recv.at[phase, group, n, by - 1],
+                    device_id=(grp, blk, planes[by]),
+                    device_id_type=MESH,
                 )
+                for by in (2, 1, 3)
+            ])
         own = [
             pltpu.make_async_copy(
                 result.at[phase, group, a, me],
@@ -274,10 +286,10 @@
             )
             for a in range(2)
         ]
-        return copies, own
+        return parts, own
 
     score_scale = 1.0 / math.sqrt(DH)
-    norm = 1.0 / math.sqrt(REACH * BLOCK)
+    both_scales = 1.0 / math.sqrt(DH * REACH * BLOCK)
     part = ROWS // TOK
 
     def unit(phase, group, slot, step, diagonal):
@@ -300,16 +312,14 @@
                 row = lax.broadcasted_iota(jnp.int32, (ROWS, TOK), 0) + step * ROWS
                 col = lax.broadcasted_iota(jnp.int32, (ROWS, TOK), 1) + p * TOK
                 allowed = allowed & ((col <= row) if group == 0 else (row <= col))
-            v = scores[:, cols] * score_scale
-            s = 1.0 / (1.0 + jnp.exp(-v))
-            active = v * s
-            slope = s + active * (1.0 - s)
-            weights.append(jnp.where(allowed, active * norm, 0.0).astype(jnp.bfloat16))
-            dscores.append(
-                jnp.where(allowed, dprob[:, cols] * slope * (norm * score_scale), 0.0).astype(
-                    jnp.bfloat16
-                )
-            )
+            raw = scores[:, cols]
+            grown = 1.0 + jnp.exp2(jnp.minimum(raw * (-score_scale * LOG2E), 115.0))
+            s = pl.reciprocal(grown, approx=True)
+            s = s * (2.0 - grown * s)
+            active = raw * s
+            slope = s + active * (score_scale - score_scale * s)
+            weights.append(jnp.where(allowed, active, 0.0).astype(jnp.bfloat16))
+            dscores.append(jnp.where(allowed, dprob[:, cols] * slope, 0.0).astype(jnp.bfloat16))
         weight = jnp.concatenate(weights, axis=1)
         dscore = jnp.concatenate(dscores, axis=1)
         first_term = lax.dot_general(dscore, other_first, NN, preferred_element_type=jnp.float32)
@@ -340,9 +350,8 @@
     def finish(phase, group):
         for a in range(2):
             for p in range(PLANES):
-                result[phase, group, a, p] = acc[group, a, p * TOK : (p + 1) * TOK, :].astype(
-                    jnp.bfloat16
-                )
+                total = acc[group, a, p * TOK : (p + 1) * TOK, :] * both_scales
+                result[phase, group, a, p] = total.astype(jnp.bfloat16)
 
     exchanges = {pg: exchange(*pg) for pg in groups}
     halos = {pg: halo(*pg) for pg in groups}
@@ -351,18 +360,37 @@
     shares = {pg: share(*pg) for pg in groups}
     gives = {pg: give(*pg) for pg in groups}
 
-    def start_exchange(pg):
-        for copy in loads[pg]:
-            copy.wait()
-        for copy in exchanges[pg]:
-            copy.start()
-
-    def arrive(pg):
-        for copy in exchanges[pg]:
-            copy.wait_recv()
-
-    def start_halo(pg):
-        for condition, copy in halos[pg]:
+    queue = [part for pg in groups for part in exchanges[pg]]
+    queue += [part for pg in groups for part in gives[pg][0]]
+    window = 3
+    issued = []
+    gone = []
+
+    def left(count):
+        for n in range(len(gone), count):
+            for copy in queue[n]:
+                copy.wait_send()
+            gone.append(n)
+
+    def issue(count, limited=True):
+        for n in range(len(issued), len(issued) + count):
+            if limited:
+                left(n - window + 1)
+            if n in (0, 2 * PARTS):
+                for group in range(2):
+                    for copy in loads[n // (2 * PARTS), group]:
+                        copy.wait()
+            for copy in queue[n]:
+                copy.start()
+            issued.append(n)
+
+    def arrive(phase, turn):
+        for part in exchanges[phase, turn]:
+            for copy in part:
+                copy.wait_recv()
+
+    def start_halo(phase, turn):
+        for condition, copy in halo(phase, order[turn]):
             pl.when(condition)(copy.start)
 
     def hand_on(pg):
@@ -387,73 +415,90 @@
 
     def start_give(pg):
         finish(*pg)
-        remote, own = gives[pg]
-        for copy in remote + own:
+        for copy in gives[pg][1]:
             copy.start()
 
     kv_a, qd_a, kv_b, qd_b = groups
-    start_exchange(kv_a)
-    start_exchange(qd_a)
-
-    arrive(kv_a)
-    start_halo(kv_a)
-    start_exchange(kv_b)
+    issue(7)
+    arrive(0, 0)
+    theirs, mine = held.at[0, order[0], 0], held.at[0, order[1], 0]
     for p in range(PLANES):
-        row = held[0, 0, 0, p, 2 * TOK :, :].astype(jnp.float32)[0:1, :]
+        numbers = theirs[p, 2 * TOK :, :]
+        mine[p, 2 * TOK :, :] = numbers
+        row = numbers.astype(jnp.float32)[0:1, :]
         seg_rows[p * TOK : (p + 1) * TOK, :] = jnp.broadcast_to(row, (TOK, TOK)).T
-        held[0, 1, 0, p, 2 * TOK :, :] = held[0, 0, 0, p, 2 * TOK :, :]
+    start_halo(0, 0)
+    issue(1)
     hand_on(kv_a)
+    hand_on(qd_a)
+    issue(3)
+
+    arrive(0, 1)
+    start_halo(0, 1)
+    issue(1)
     near(kv_a)
-
-    arrive(qd_a)
-    start_halo(qd_a)
-    start_exchange(qd_b)
     diagonal(*kv_a)
+    issue(1)
     far(kv_a)
-    hand_on(qd_a)
+    issue(1)
     others(*kv_a)
     start_give(kv_a)
+    issue(2)
+
+    arrive(1, 0)
+    start_halo(1, 0)
     near(qd_a)
     diagonal(*qd_a)
+    hand_on(kv_b)
+    hand_on(qd_b)
+    issue(1)
     far(qd_a)
     others(*qd_a)
     start_give(qd_a)
-
-    arrive(kv_b)
-    start_halo(kv_b)
-    hand_on(kv_b)
+    issue(2)
+
+    arrive(1, 1)
+    start_halo(1, 1)
     near(kv_b)
-    arrive(qd_b)
-    start_halo(qd_b)
     diagonal(*kv_b)
+    issue(6 * PARTS - len(issued), limited=False)
     far(kv_b)
-    hand_on(qd_b)
     others(*kv_b)
     start_give(kv_b)
+    issue(PARTS, limited=False)
+
     near(qd_b)
     diagonal(*qd_b)
     far(qd_b)
     others(*qd_b)
     start_give(qd_b)
-
+    issue(PARTS, limited=False)
+
+    left(len(queue))
     for pg in groups:
-        for copy in exchanges[pg] + shares[pg]:
+        for copy in shares[pg]:
             copy.wait_send()
         for condition, copy in halos[pg] + [passed[pg], seconds[pg]]:
             pl.when(condition)(copy.wait_send)
     for pg in groups:
-        remote, own = gives[pg]
-        for copy in remote + own:
+        parts, own = gives[pg]
+        for part in parts:
+            for copy in part:
+                copy.wait_recv()
+        for copy in own:
             copy.wait()
 
 
 def hand_over(*refs):
-    copies = [
-        pltpu.make_async_copy(refs[i], refs[4 + i], refs[8].at[i]) for i in range(4)
-    ]
-    for copy in copies:
+    ins, outs, (here, sems) = refs[:4], refs[4:8], refs[8:]
+    arriving = [pltpu.make_async_copy(ins[i], here.at[i], sems.at[0, i]) for i in range(4)]
+    leaving = [pltpu.make_async_copy(here.at[i], outs[i], sems.at[1, i]) for i in range(4)]
+    for copy in arriving:
         copy.start()
-    for copy in copies:
+    for i in range(4):
+        arriving[i].wait()
+        leaving[i].start()
+    for copy in leaving:
         copy.wait()
 
 
@@ -474,14 +519,14 @@
             pltpu.VMEM((2, 2, BLOCK, DH), jnp.float32),
             pltpu.VMEM((BLOCK, TOK), jnp.float32),
             dma((2, 2, PLANES, 2)),
-            dma((2, 2, 3)),
-            dma((2, 2, 3)),
+            dma((2, 2, PARTS, 3)),
+            dma((2, 2, PARTS, 3)),
             dma((2, 2, 2)),
             dma((2, 2, 2)),
             dma((2, 2, 2)),
             dma((2, 2, 2)),
-            dma((2, 2, 2, 3)),
-            dma((2, 2, 2, 3)),
+            dma((2, 2, PARTS, 3)),
+            dma((2, 2, PARTS, 3)),
             dma((2, 2, 2)),
             pltpu.VMEM((2, 2, CHUNK, DH), jnp.bfloat16),
             dma((2, 2, SIDE)),
@@ -505,7 +550,7 @@
         out_shape=(shape,) * 4,
         in_specs=[anywhere] * 4,
         out_specs=[anywhere] * 4,
-        scratch_shapes=[dma((4,))],
+        scratch_shapes=[pltpu.VMEM((4, tokens, features), jnp.bfloat16), dma((2, 4))],
         compiler_params=pltpu.CompilerParams(vmem_limit_bytes=60 << 20),
     )(*results)
 

time: 183 us -> 137 us (0.75)
  the two profiles are of different devices: /device:TPU:55 before, /device:TPU:81 now
where the time goes in v2:
time: 137 us
  Pallas kernels  136 us (99%)
    pallas_call x1, Pallas kernels, shards(): pl.pallas_call(functools.partial(kernel, grps), out_shape=(shape,) * 4, i...  134 us

profile of v2, /device:TPU:81, one launch (start us, length us, event | category | flops | bytes accessed | tf_op | source)
XLA Modules:
  0.0 136.6 jit_solution(8935304423200786503)
XLA Ops:
  0.6 134.0 %shard_map.84 = (bf16[128,1024]{1,0:T(8,128)(2,1)}, bf16[128,1024]{1,0:T(8,128)(2,1)}, bf16[128,1024]{1,0:T(8,128)(2,1)}, bf16[128,1024]{1,0:T(8,128)(2,1)}) custom-call(bf16[128,1024]{1,0:T(8,128)(2,1)} %queries.1, bf16[128,1024]{1,0:T(8,128)(2,1)} %keys.1, bf16[128,1024]{1,0:T(8,128)(2,1)} %values.1, bf16[128,1024]{1,0:T(8,128)(2,1)} %out_grad.1, ...), custom_call_target="tpu_custom_call" | custom-call | flops 5368709120 | bytes 2097152 | tf_op jit(solution)/shard_map/pallas_call | solution.py:510
  134.6 2.0 %shard_map.85 = (bf16[128,1024]{1,0:T(8,128)(2,1)}, bf16[128,1024]{1,0:T(8,128)(2,1)}, bf16[128,1024]{1,0:T(8,128)(2,1)}, bf16[128,1024]{1,0:T(8,128)(2,1)}) custom-call(bf16[128,1024]{1,0:T(8,128)(2,1)} %get-tuple-element.8.refs_0_, bf16[128,1024]{1,0:T(8,128)(2,1)} %get-tuple-element.9.refs_1_, bf16[128,1024]{1,0:T(8,128)(2,1)} %get-tuple-element.10.refs_2_, ...), custom_call_target="tpu_custom_call" | custom-call | tf_op jit(solution)/shard_map/pallas_call | solution.py:548

commit v3 on v2

--- a/solution.py
+++ b/solution.py
@@ -61,8 +61,8 @@
 
     last = (SIDE - 1, SIDE - 1)
 
-    first = jnp.where(chip(1)[3] <= 1, 1, 0)
-    order = (first, 1 - first)
+    first = jnp.where((chip(1)[3] <= 1) & (grp >= 1), 1, 0)
+    order = ((0, 1), (first, 1 - first))
 
     sources = ((keys, values), (queries, out_grad))
     groups = ((0, 0), (0, 1), (1, 0), (1, 1))
@@ -115,15 +115,17 @@
         for by in (1, 2):
             greeted += greet_if(k >= by, [device(group, chip_place(g, k - by))])
             greeted += greet_if(k < CHIPS - by, [device(group, chip_place(g, k + by))])
-        relays = (y <= 1) & (g >= 1)
         greeted += greet_if(
-            relays & (x == 0), [device(group, (g, p, y)) for p in range(1, SIDE)]
+            (x == 0) & (y <= 1) & (g >= 1),
+            [device(group, (g, p, y)) for p in range(1, SIDE)]
+            + [device(group, (g, p, SIDE - 1 - y)) for p in range(SIDE)],
         )
-        greeted += greet_if(relays & (x > 0), [device(group, (g, 0, y))])
-        greeted += greet_if(relays, [device(group, (g - 1, *last))])
+        greeted += greet_if((x > 0) & (y <= 1) & (g >= 1), [device(group, (g, 0, y))])
+        greeted += greet_if((y >= 2) & (g >= 1), [device(group, (g, 0, SIDE - 1 - y))])
+        greeted += greet_if(g >= 1, [device(group, (g - 1, *last))])
         greeted += greet_if(
             (k == CHIPS - 1) & (g < grps - 1),
-            [device(group, (g + 1, p, row)) for p in range(SIDE) for row in range(2)],
+            [device(group, (g + 1, p, row)) for p in range(SIDE) for row in range(SIDE)],
         )
 
     def blank(group, slot):
@@ -143,15 +145,14 @@
 
     seg_load.wait()
     seg = jnp.broadcast_to(seg_here[...].astype(jnp.float32), (16, TOK)).astype(jnp.bfloat16)
-    for group in range(2):
-        for by in range(3):
-            stage[0, group, by, 2 * TOK :, :] = seg
-        held[0, group, 0, me, 2 * TOK :, :] = seg
+    for by in range(3):
+        stage[0, 0, by, 2 * TOK :, :] = seg
+    held[0, 0, 0, me, 2 * TOK :, :] = seg
 
     pl.semaphore_wait(barrier, greeted)
 
     def exchange(phase, turn):
-        group = order[turn]
+        group = order[phase][turn]
         total = CHUNK if phase == turn == 0 else 2 * TOK
         parts = []
         for n in range(PARTS):
@@ -169,8 +170,8 @@
             ])
         return parts
 
-    def block_rows(phase):
-        return pl.ds(0, CHUNK if phase == 0 else 2 * TOK)
+    def block_rows(phase, a):
+        return pl.ds(a * TOK, CHUNK - TOK if phase == 0 and a == 1 else TOK)
 
     def send(source, to, send_sem, recv_sem, device_id):
         return pltpu.make_async_remote_copy(
@@ -182,8 +183,8 @@
             device_id_type=MESH,
         )
 
-    def halo(phase, group):
-        rows = block_rows(phase)
+    def halo(phase, group, a):
+        rows = block_rows(phase, a)
         g, x, y, k = chip(group)
         copies = []
         for by in (1, 2):
@@ -192,70 +193,71 @@
                 send(
                     held.at[phase, group, 0, :, rows],
                     held.at[phase, group, 2 * by, :, rows],
-                    halo_send.at[phase, group, by - 1],
-                    halo_recv.at[phase, group, by - 1],
+                    halo_send.at[phase, group, a, by - 1],
+                    halo_recv.at[phase, group, a, by - 1],
                     device(group, chip_place(g, jnp.maximum(k - by, 0))),
                 ),
             ))
         edge = (k <= 1) & (g >= 1)
         near_row = jnp.minimum(y, 1)
-        for p in range(1, SIDE):
+        for p in range(1 - a, SIDE):
             copies.append((
                 edge,
                 send(
                     held.at[phase, group, 0, p, rows],
                     relay.at[phase, group, rows],
-                    piece_send.at[phase, group, p],
+                    piece_send.at[phase, group, a, p],
                     relay_recv.at[phase, group],
-                    device(group, (g, p, y)),
+                    device(group, (g, p, SIDE - 1 - y if a else y)),
                 ),
             ))
-        copies.append((
-            edge,
-            send(
-                held.at[phase, group, 0, 0, rows],
-                held.at[phase, group, 2 * (near_row + 1), 0, rows],
-                piece_send.at[phase, group, 0],
-                halo_recv.at[phase, group, near_row],
-                device(group, (jnp.maximum(g - 1, 0), *last)),
-            ),
-        ))
+        if a == 0:
+            copies.append((
+                edge,
+                send(
+                    held.at[phase, group, 0, 0, rows],
+                    held.at[phase, group, 2 * (near_row + 1), 0, rows],
+                    piece_send.at[phase, group, 0, 0],
+                    halo_recv.at[phase, group, 0, near_row],
+                    device(group, (jnp.maximum(g - 1, 0), *last)),
+                ),
+            ))
         return copies
 
-    def pass_piece(phase, group):
-        rows = block_rows(phase)
+    def pass_piece(phase, group, a):
+        rows = block_rows(phase, a)
         g, x, y, k = chip(group)
-        near_row = jnp.minimum(y, 1)
-        return (x >= 1) & (y <= 1) & (g >= 1), send(
+        near_row = jnp.clip(SIDE - 1 - y if a else y, 0, 1)
+        condition = (y >= 2) if a else (y <= 1) & (x >= 1)
+        return condition & (g >= 1), send(
             relay.at[phase, group, rows],
             held.at[phase, group, 2 * (near_row + 1), x, rows],
             relay_send.at[phase, group],
-            halo_recv.at[phase, group, near_row],
+            halo_recv.at[phase, group, a, near_row],
             device(group, (jnp.maximum(g - 1, 0), *last)),
         )
 
-    def pass_block(phase, group):
-        rows = block_rows(phase)
+    def pass_block(phase, group, a):
+        rows = block_rows(phase, a)
         g, x, y, k = chip(group)
         return (k == CHIPS - 1) & (g < grps - 1), send(
             held.at[phase, group, 2, :, rows],
             held.at[phase, group, 4, :, rows],
-            next_send.at[phase, group],
-            halo_recv.at[phase, group, 1],
+            next_send.at[phase, group, a],
+            halo_recv.at[phase, group, a, 1],
             device(group, (g, SIDE - 1, SIDE - 2)),
         )
 
-    def share(phase, group):
-        rows = block_rows(phase)
+    def share(phase, group, a):
+        rows = block_rows(phase, a)
         side = core if group == 0 else 1 - core
         return [
-            pltpu.make_async_remote_copy(
-                src_ref=held.at[phase, group, 2 * j + 2 * side, :, rows],
-                dst_ref=held.at[phase, group, 2 * j + 1, :, rows],
-                send_sem=sib_send.at[phase, group, j],
-                recv_sem=sib_recv.at[phase, group, j],
-                device_id=sibling,
-                device_id_type=MESH,
+            send(
+                held.at[phase, group, 2 * j + 2 * side, :, rows],
+                held.at[phase, group, 2 * j + 1, :, rows],
+                sib_send.at[phase, group, a, j],
+                sib_recv.at[phase, group, a, j],
+                sibling,
             )
             for j in range(2)
         ]
@@ -354,10 +356,11 @@
                 result[phase, group, a, p] = total.astype(jnp.bfloat16)
 
     exchanges = {pg: exchange(*pg) for pg in groups}
-    halos = {pg: halo(*pg) for pg in groups}
-    passed = {pg: pass_piece(*pg) for pg in groups}
-    seconds = {pg: pass_block(*pg) for pg in groups}
-    shares = {pg: share(*pg) for pg in groups}
+    halves = [(*pg, a) for pg in groups for a in range(2)]
+    halos = {half: halo(*half) for half in halves}
+    passed = {half: pass_piece(*half) for half in halves}
+    seconds = {half: pass_block(*half) for half in halves}
+    shares = {half: share(*half) for half in halves}
     gives = {pg: give(*pg) for pg in groups}
 
     queue = [part for pg in groups for part in exchanges[pg]]
@@ -384,34 +387,46 @@
                 copy.start()
             issued.append(n)
 
-    def arrive(phase, turn):
-        for part in exchanges[phase, turn]:
+    def arrive(phase, turn, a):
+        for part in exchanges[phase, turn][a * PARTS // 2 : (a + 1) * PARTS // 2]:
             for copy in part:
                 copy.wait_recv()
 
-    def start_halo(phase, turn):
-        for condition, copy in halo(phase, order[turn]):
+    def start_halo(phase, turn, a):
+        for condition, copy in halo(phase, order[phase][turn], a):
             pl.when(condition)(copy.start)
 
     def hand_on(pg):
-        condition, copy = passed[pg]
-
-        @pl.when(condition)
-        def _():
-            pltpu.make_async_copy(copy.src_ref, copy.src_ref, relay_recv.at[pg]).wait()
-            copy.start()
+        for a in range(2):
+            condition, copy = passed[*pg, a]
+
+            @pl.when(condition)
+            def _():
+                pltpu.make_async_copy(copy.src_ref, copy.src_ref, relay_recv.at[pg]).wait()
+                copy.start()
+
+    def forward(pg):
+        for a in range(2):
+            condition, copy = seconds[*pg, a]
+
+            @pl.when(condition)
+            def _():
+                halos[*pg, a][0][1].wait_recv()
+                copy.start()
 
     def near(pg):
-        pl.when(comes(pg[1], 1))(halos[pg][0][1].wait_recv)
-        condition, copy = seconds[pg]
-        pl.when(condition)(copy.start)
-        shares[pg][0].start()
+        for a in range(2):
+            inside = comes(pg[1], 1) & ~seconds[*pg, a][0]
+            pl.when(inside)(halos[*pg, a][0][1].wait_recv)
+            shares[*pg, a][0].start()
 
     def far(pg):
-        pl.when(comes(pg[1], 2))(halos[pg][1][1].wait_recv)
-        shares[pg][1].start()
-        for copy in shares[pg]:
-            copy.wait_recv()
+        for a in range(2):
+            pl.when(comes(pg[1], 2))(halos[*pg, a][1][1].wait_recv)
+            shares[*pg, a][1].start()
+        for a in range(2):
+            for copy in shares[*pg, a]:
+                copy.wait_recv()
 
     def start_give(pg):
         finish(*pg)
@@ -419,48 +434,62 @@
             copy.start()
 
     kv_a, qd_a, kv_b, qd_b = groups
-    issue(7)
-    arrive(0, 0)
-    theirs, mine = held.at[0, order[0], 0], held.at[0, order[1], 0]
+    issue(5)
+    arrive(0, 0, 0)
+    start_halo(0, 0, 0)
+    issue(2)
+    arrive(0, 0, 1)
+    theirs, mine = held.at[0, 0, 0], held.at[0, 1, 0]
     for p in range(PLANES):
         numbers = theirs[p, 2 * TOK :, :]
         mine[p, 2 * TOK :, :] = numbers
         row = numbers.astype(jnp.float32)[0:1, :]
         seg_rows[p * TOK : (p + 1) * TOK, :] = jnp.broadcast_to(row, (TOK, TOK)).T
-    start_halo(0, 0)
+    start_halo(0, 0, 1)
     issue(1)
     hand_on(kv_a)
-    hand_on(qd_a)
-    issue(3)
-
-    arrive(0, 1)
-    start_halo(0, 1)
+    issue(2)
+    arrive(0, 1, 0)
+    start_halo(0, 1, 0)
     issue(1)
+    arrive(0, 1, 1)
+    start_halo(0, 1, 1)
+
+    issue(1)
+    forward(kv_a)
     near(kv_a)
     diagonal(*kv_a)
+    hand_on(qd_a)
     issue(1)
     far(kv_a)
     issue(1)
+    arrive(1, 0, 0)
+    start_halo(1, 0, 0)
     others(*kv_a)
     start_give(kv_a)
     issue(2)
 
-    arrive(1, 0)
-    start_halo(1, 0)
+    arrive(1, 0, 1)
+    start_halo(1, 0, 1)
+    forward(qd_a)
     near(qd_a)
     diagonal(*qd_a)
     hand_on(kv_b)
     hand_on(qd_b)
     issue(1)
     far(qd_a)
+    arrive(1, 1, 0)
+    start_halo(1, 1, 0)
     others(*qd_a)
     start_give(qd_a)
     issue(2)
 
-    arrive(1, 1)
-    start_halo(1, 1)
+    arrive(1, 1, 1)
+    start_halo(1, 1, 1)
+    forward(kv_b)
     near(kv_b)
     diagonal(*kv_b)
+    forward(qd_b)
     issue(6 * PARTS - len(issued), limited=False)
     far(kv_b)
     others(*kv_b)
@@ -475,10 +504,10 @@
     issue(PARTS, limited=False)
 
     left(len(queue))
-    for pg in groups:
-        for copy in shares[pg]:
+    for half in halves:
+        for copy in shares[half]:
             copy.wait_send()
-        for condition, copy in halos[pg] + [passed[pg], seconds[pg]]:
+        for condition, copy in halos[half] + [passed[half], seconds[half]]:
             pl.when(condition)(copy.wait_send)
     for pg in groups:
         parts, own = gives[pg]
@@ -521,18 +550,18 @@
             dma((2, 2, PLANES, 2)),
             dma((2, 2, PARTS, 3)),
             dma((2, 2, PARTS, 3)),
-            dma((2, 2, 2)),
-            dma((2, 2, 2)),
-            dma((2, 2, 2)),
-            dma((2, 2, 2)),
+            dma((2, 2, 2, 2)),
+            dma((2, 2, 2, 2)),
+            dma((2, 2, 2, 2)),
+            dma((2, 2, 2, 2)),
             dma((2, 2, PARTS, 3)),
             dma((2, 2, PARTS, 3)),
             dma((2, 2, 2)),
             pltpu.VMEM((2, 2, CHUNK, DH), jnp.bfloat16),
-            dma((2, 2, SIDE)),
+            dma((2, 2, 2, SIDE)),
             dma((2, 2)),
             dma((2, 2)),
-            dma((2, 2)),
+            dma((2, 2, 2)),
             dma(()),
             pltpu.VMEM((1, TOK), jnp.int32),
         ],

time: 137 us -> 129 us (0.942)
  the two profiles are of different devices: /device:TPU:81 before, /device:TPU:41 now
where the time goes in v3:
time: 129 us
  Pallas kernels  128 us (99%)
    pallas_call x1, Pallas kernels, shards(): pl.pallas_call(functools.partial(kernel, grps), out_shape=(shape,) * 4, i...  126 us

profile of v3, /device:TPU:41, one launch (start us, length us, event | category | flops | bytes accessed | tf_op | source)
XLA Modules:
  0.0 128.7 jit_solution(617299425362224773)
XLA Ops:
  0.6 126.0 %shard_map.84 = (bf16[128,1024]{1,0:T(8,128)(2,1)}, bf16[128,1024]{1,0:T(8,128)(2,1)}, bf16[128,1024]{1,0:T(8,128)(2,1)}, bf16[128,1024]{1,0:T(8,128)(2,1)}) custom-call(bf16[128,1024]{1,0:T(8,128)(2,1)} %queries.1, bf16[128,1024]{1,0:T(8,128)(2,1)} %keys.1, bf16[128,1024]{1,0:T(8,128)(2,1)} %values.1, bf16[128,1024]{1,0:T(8,128)(2,1)} %out_grad.1, ...), custom_call_target="tpu_custom_call" | custom-call | flops 5368709120 | bytes 2097152 | tf_op jit(solution)/shard_map/pallas_call | solution.py:539
  126.7 2.0 %shard_map.85 = (bf16[128,1024]{1,0:T(8,128)(2,1)}, bf16[128,1024]{1,0:T(8,128)(2,1)}, bf16[128,1024]{1,0:T(8,128)(2,1)}, bf16[128,1024]{1,0:T(8,128)(2,1)}) custom-call(bf16[128,1024]{1,0:T(8,128)(2,1)} %get-tuple-element.8.refs_0_, bf16[128,1024]{1,0:T(8,128)(2,1)} %get-tuple-element.9.refs_1_, bf16[128,1024]{1,0:T(8,128)(2,1)} %get-tuple-element.10.refs_2_, ...), custom_call_target="tpu_custom_call" | custom-call | tf_op jit(solution)/shard_map/pallas_call | solution.py:577

commit v4 on v3

--- a/solution.py
+++ b/solution.py
@@ -342,12 +342,12 @@
 
         lax.fori_loop(0, steps, body, 0)
 
-    def others(phase, group):
+    def others(phase, group, upper):
         def body(i, carry):
-            unit(phase, group, 1 + i // steps, lax.rem(i, steps), False)
+            unit(phase, group, upper - i // steps, lax.rem(i, steps), False)
             return carry
 
-        lax.fori_loop(0, REACH * steps, body, 0)
+        lax.fori_loop(0, 2 * steps, body, 0)
 
     def finish(phase, group):
         for a in range(2):
@@ -420,13 +420,19 @@
             pl.when(inside)(halos[*pg, a][0][1].wait_recv)
             shares[*pg, a][0].start()
 
+    def middle(pg):
+        diagonal(*pg)
+        for a in range(2):
+            shares[*pg, a][0].wait_recv()
+        others(*pg, 2)
+
     def far(pg):
         for a in range(2):
             pl.when(comes(pg[1], 2))(halos[*pg, a][1][1].wait_recv)
             shares[*pg, a][1].start()
         for a in range(2):
-            for copy in shares[*pg, a]:
-                copy.wait_recv()
+            shares[*pg, a][1].wait_recv()
+        others(*pg, 4)
 
     def start_give(pg):
         finish(*pg)
@@ -458,14 +464,12 @@
     issue(1)
     forward(kv_a)
     near(kv_a)
-    diagonal(*kv_a)
     hand_on(qd_a)
-    issue(1)
-    far(kv_a)
-    issue(1)
+    middle(kv_a)
+    issue(2)
     arrive(1, 0, 0)
     start_halo(1, 0, 0)
-    others(*kv_a)
+    far(kv_a)
     start_give(kv_a)
     issue(2)
 
@@ -473,14 +477,13 @@
     start_halo(1, 0, 1)
     forward(qd_a)
     near(qd_a)
-    diagonal(*qd_a)
+    middle(qd_a)
     hand_on(kv_b)
     hand_on(qd_b)
     issue(1)
-    far(qd_a)
     arrive(1, 1, 0)
     start_halo(1, 1, 0)
-    others(*qd_a)
+    far(qd_a)
     start_give(qd_a)
     issue(2)
 
@@ -488,18 +491,16 @@
     start_halo(1, 1, 1)
     forward(kv_b)
     near(kv_b)
-    diagonal(*kv_b)
+    middle(kv_b)
     forward(qd_b)
     issue(6 * PARTS - len(issued), limited=False)
     far(kv_b)
-    others(*kv_b)
     start_give(kv_b)
     issue(PARTS, limited=False)
 
     near(qd_b)
-    diagonal(*qd_b)
+    middle(qd_b)
     far(qd_b)
-    others(*qd_b)
     start_give(qd_b)
     issue(PARTS, limited=False)
 

time: 129 us -> 126 us (0.977)
  Pallas kernels: 128 us -> 125 us
    pallas_call x1, Pallas kernels: 126 us -> 123 us  [shards(): pl.pallas_call(functools.partial(kernel, grps), out_shape=(shape,) * 4, i...]
where the time goes in v4:
time: 126 us
  Pallas kernels  125 us (99%)
    pallas_call x1, Pallas kernels, shards(): pl.pallas_call(functools.partial(kernel, grps), out_shape=(shape,) * 4, i...  123 us

profile of v4, /device:TPU:41, one launch (start us, length us, event | category | flops | bytes accessed | tf_op | source)
XLA Modules:
  0.0 125.7 jit_solution(12530866499695366193)
XLA Ops:
  0.6 122.9 %shard_map.84 = (bf16[128,1024]{1,0:T(8,128)(2,1)}, bf16[128,1024]{1,0:T(8,128)(2,1)}, bf16[128,1024]{1,0:T(8,128)(2,1)}, bf16[128,1024]{1,0:T(8,128)(2,1)}) custom-call(bf16[128,1024]{1,0:T(8,128)(2,1)} %queries.1, bf16[128,1024]{1,0:T(8,128)(2,1)} %keys.1, bf16[128,1024]{1,0:T(8,128)(2,1)} %values.1, bf16[128,1024]{1,0:T(8,128)(2,1)} %out_grad.1, ...), custom_call_target="tpu_custom_call" | custom-call | flops 5368709120 | bytes 2097152 | tf_op jit(solution)/shard_map/pallas_call | solution.py:540
  123.5 2.0 %shard_map.85 = (bf16[128,1024]{1,0:T(8,128)(2,1)}, bf16[128,1024]{1,0:T(8,128)(2,1)}, bf16[128,1024]{1,0:T(8,128)(2,1)}, bf16[128,1024]{1,0:T(8,128)(2,1)}) custom-call(bf16[128,1024]{1,0:T(8,128)(2,1)} %get-tuple-element.8.refs_0_, bf16[128,1024]{1,0:T(8,128)(2,1)} %get-tuple-element.9.refs_1_, bf16[128,1024]{1,0:T(8,128)(2,1)} %get-tuple-element.10.refs_2_, ...), custom_call_target="tpu_custom_call" | custom-call | tf_op jit(solution)/shard_map/pallas_call | solution.py:578

commit v5 on v4

--- a/solution.py
+++ b/solution.py
@@ -471,10 +471,10 @@
     start_halo(1, 0, 0)
     far(kv_a)
     start_give(kv_a)
-    issue(2)
-
     arrive(1, 0, 1)
     start_halo(1, 0, 1)
+    issue(2)
+
     forward(qd_a)
     near(qd_a)
     middle(qd_a)

time: 126 us -> 127 us (level)
  the two profiles are of different devices: /device:TPU:41 before, /device:TPU:17 now
where the time goes in v5:
time: 127 us
  Pallas kernels  126 us (99%)
    pallas_call x1, Pallas kernels, shards(): pl.pallas_call(functools.partial(kernel, grps), out_shape=(shape,) * 4, i...  124 us

profile of v5, /device:TPU:17, one launch (start us, length us, event | category | flops | bytes accessed | tf_op | source)
XLA Modules:
  0.0 126.8 jit_solution(11310690043025808603)
XLA Ops:
  0.6 124.0 %shard_map.84 = (bf16[128,1024]{1,0:T(8,128)(2,1)}, bf16[128,1024]{1,0:T(8,128)(2,1)}, bf16[128,1024]{1,0:T(8,128)(2,1)}, bf16[128,1024]{1,0:T(8,128)(2,1)}) custom-call(bf16[128,1024]{1,0:T(8,128)(2,1)} %queries.1, bf16[128,1024]{1,0:T(8,128)(2,1)} %keys.1, bf16[128,1024]{1,0:T(8,128)(2,1)} %values.1, bf16[128,1024]{1,0:T(8,128)(2,1)} %out_grad.1, ...), custom_call_target="tpu_custom_call" | custom-call | flops 5368709120 | bytes 2097152 | tf_op jit(solution)/shard_map/pallas_call | solution.py:540
  124.7 2.0 %shard_map.85 = (bf16[128,1024]{1,0:T(8,128)(2,1)}, bf16[128,1024]{1,0:T(8,128)(2,1)}, bf16[128,1024]{1,0:T(8,128)(2,1)}, bf16[128,1024]{1,0:T(8,128)(2,1)}) custom-call(bf16[128,1024]{1,0:T(8,128)(2,1)} %get-tuple-element.8.refs_0_, bf16[128,1024]{1,0:T(8,128)(2,1)} %get-tuple-element.9.refs_1_, bf16[128,1024]{1,0:T(8,128)(2,1)} %get-tuple-element.10.refs_2_, ...), custom_call_target="tpu_custom_call" | custom-call | tf_op jit(solution)/shard_map/pallas_call | solution.py:578
